TPU v7x, 32 devices: a whole 2x2x4 slice. The times are simulated.
32 devices in a mesh: ens: 2 (over y), lon: 4 (over z), lat: 2 (over x), ch: 2 (over core).
Axes of the slice: x: 2, y: 2, z: 4, core: 2. Of those that a mesh axis runs over, the one named last changes fastest.
Arguments:
- features: bfloat16 [64, 64, 256], P(('ens', 'lat'), 'lon', 'ch'), parts along dimension 0, may hold values from -6 to 6
- basis: bfloat16 [9, 32, 7, 9], replicated, may hold values from -0.8984375 to 0.8984375
- active: int32 [32, 7], replicated, may hold values from 0 to 1, as said below
- reach: int32 [32], replicated, may hold values from 1 to 4, as said below
- weight: bfloat16 [9, 256, 256], P(None, 'ch'), may hold values from -0.125 to 0.125
- cotangent: bfloat16 [64, 64, 256], P(('ens', 'lat'), 'lon', 'ch'), parts along dimension 0, may hold values from -3 to 3
Outputs:
- output: bfloat16 [64, 64, 256], P(('ens', 'lat'), 'lon', 'ch'), parts along dimension 0
- input_grad: bfloat16 [64, 64, 256], P(('ens', 'lat'), 'lon', 'ch'), parts along dimension 0
- weight_grad: float32 [18, 256, 256], P('ens', 'ch'), parts along dimension 0
There are 2 independent parts, one for each index of `ens`. A program takes and returns all parts, laid end to end along the dimension named above; an argument that names none is the same for every part. Nothing has to cross between parts.
Inputs may be any that keep to these rules, and one draw needn't show every extreme that they name: `active`: 1 at offset 3 in every row, and at every offset in the first and last 8 rows. `reach`: equal to 4 in the first and last 8 rows.
All inputs are finite; a program needn't handle non-finite values.
Results may differ from a plain program's by a relative error of at most 0.0049.
Values may be sent and summed in bfloat16 or wider, within the bound.
A program may use at most 64 MiB of HBM per device.

v0:
```python
import jax
import jax.numpy as jnp
from jax import lax
from jax.sharding import PartitionSpec as P


def with_halo(cells, sides, width, closed):
    for axis, dim in sides:
        count = lax.axis_size(axis)
        ends = count if closed else count - 1
        head = lax.slice_in_dim(cells, 0, width, axis=dim)
        tail = lax.slice_in_dim(cells, cells.shape[dim] - width, cells.shape[dim], axis=dim)
        cells = jnp.concatenate(
            [
                lax.ppermute(tail, axis, [(i, (i + 1) % count) for i in range(ends)]),
                cells,
                lax.ppermute(head, axis, [((i + 1) % count, i) for i in range(ends)]),
            ],
            axis=dim,
        )
    return cells


def passed_along(value, axis, steps):
    count = lax.axis_size(axis)
    pairs = [(source, (source + steps) % count) for source in range(count)]
    return lax.ppermute(value, axis, pairs)


def shifted(value, axis, steps):
    count = lax.axis_size(axis)
    initial, last = (max(0, -steps), min(count, count - steps))
    return lax.ppermute(value, axis, [(source, source + steps) for source in range(initial, last)])


def live_basis(basis, active, reach, lon_half):
    distance = jnp.abs(jnp.arange(2 * lon_half + 1, dtype=jnp.int32) - lon_half)
    lon_live = (distance[None, :] <= reach[:, None]).astype(jnp.int32)
    live_mask = active[:, :, None] * lon_live[:, None, :]
    return basis * live_mask[None].astype(basis.dtype)


def body(features, basis, active, reach, weight, cotangent):
    lat_rows, lon_cols, channels = features.shape
    kernels = basis.shape[0]
    lat_span = basis.shape[2]
    lon_span = basis.shape[3]
    lat_half = (lat_span - 1) // 2
    lon_half = (lon_span - 1) // 2
    ext_width = lon_cols + 2 * lon_half
    out_width = weight.shape[2]
    contract = (((2,), (1,)), ((0,), (0,)))
    first_row = lax.axis_index("lat") * lat_rows
    masked = live_basis(basis, active, reach, lon_half)
    padded_basis = jnp.pad(masked, ((0, 0), (lat_half, lat_half), (0, 0), (0, 0)))
    band_basis = lax.dynamic_slice_in_dim(padded_basis, first_row, lat_rows + 2 * lat_half, 1)
    own_basis = band_basis[:, lat_half : lat_half + lat_rows]
    place = (
        jnp.arange(ext_width)[None, None, :]
        == jnp.arange(lon_cols)[None, :, None] + jnp.arange(lon_span)[:, None, None]
    )
    shift_table = place.astype(jnp.bfloat16)
    tiles = jnp.einsum(
        "kiab,bjq->ijkaq", own_basis, shift_table, preferred_element_type=jnp.float32
    )
    tiles = tiles.astype(jnp.bfloat16).reshape(lat_rows, lon_cols * kernels, lat_span, ext_width)
    lon_ext = with_halo(features, (("lon", 1),), lon_half, True)
    extended = with_halo(lon_ext, (("lat", 0),), lat_half, False)
    windows = jnp.stack(
        [extended[offset : offset + lat_rows] for offset in range(lat_span)], axis=1
    )
    windows = windows.reshape(lat_rows, lat_span * ext_width, channels)
    running = lax.dot_general(
        tiles.reshape(lat_rows, lon_cols * kernels, lat_span * ext_width),
        windows,
        contract,
        preferred_element_type=jnp.float32,
    )
    mixed = running.astype(jnp.bfloat16).reshape(lat_rows, lon_cols, kernels, channels)
    flat = mixed.reshape(lat_rows * lon_cols, kernels * channels)
    partial_out = jnp.dot(
        flat, weight.reshape(kernels * channels, out_width), preferred_element_type=jnp.float32
    ).reshape(lat_rows, lon_cols, out_width)
    output = lax.psum_scatter(partial_out, "ch", scatter_dimension=2, tiled=True).astype(
        jnp.bfloat16
    )
    full_cot = lax.all_gather(cotangent, "ch", axis=2, tiled=True)
    flat_cot = full_cot.reshape(lat_rows * lon_cols, out_width)
    grad_local = lax.dot_general(
        flat, flat_cot, (((0,), (0,)), ((), ())), preferred_element_type=jnp.float32
    )
    weight_grad = lax.psum(grad_local, ("lon", "lat")).reshape(kernels, channels, out_width)
    spread = jnp.einsum(
        "ijo,kco->ijkc", full_cot, weight, preferred_element_type=jnp.float32
    ).astype(jnp.bfloat16)
    contrib = lax.dot_general(
        tiles.reshape(lat_rows, lon_cols * kernels, lat_span * ext_width),
        spread.reshape(lat_rows, lon_cols * kernels, channels),
        (((1,), (1,)), ((0,), (0,))),
        preferred_element_type=jnp.float32,
    )
    contrib = contrib.reshape(lat_rows, lat_span, ext_width, channels)
    spread_rows = jnp.zeros((lat_rows + 2 * lat_half, ext_width, channels), jnp.float32)
    for offset in range(lat_span):
        spread_rows = spread_rows.at[offset : offset + lat_rows].add(contrib[:, offset])
    from_right = passed_along(spread_rows[:, :lon_half].astype(jnp.bfloat16), "lon", -1).astype(
        jnp.float32
    )
    from_left = passed_along(
        spread_rows[:, lon_half + lon_cols :].astype(jnp.bfloat16), "lon", 1
    ).astype(jnp.float32)
    interior = spread_rows[:, lon_half : lon_half + lon_cols]
    interior = interior.at[:, lon_cols - lon_half :].add(from_right)
    interior = interior.at[:, :lon_half].add(from_left)
    from_below = shifted(interior[:lat_half], "lat", -1)
    from_above = shifted(interior[lat_half + lat_rows :], "lat", 1)
    band_core = interior[lat_half : lat_half + lat_rows]
    band_core = band_core.at[lat_rows - lat_half :].add(from_below)
    band_core = band_core.at[:lat_half].add(from_above)
    return (output, band_core.astype(jnp.bfloat16), weight_grad)


def solution(mesh):
    return jax.shard_map(
        body,
        mesh=mesh,
        in_specs=(
            P(("ens", "lat"), "lon", "ch"),
            P(),
            P(),
            P(),
            P(None, "ch", None),
            P(("ens", "lat"), "lon", "ch"),
        ),
        out_specs=(
            P(("ens", "lat"), "lon", "ch"),
            P(("ens", "lat"), "lon", "ch"),
            P("ens", "ch", None),
        ),
        check_vma=False,
    )
```

profile of v0, /device:TPU:0, one launch (start us, length us, event | category | flops | bytes accessed | tf_op | source)
XLA Modules:
  0.0 140.8 jit_solution(3931548292027103501)
XLA Ops:
  8.0 0.0 copy-start
  8.0 0.0 reduce-scatter.2.cloned.1.call-start
  8.1 1.5 %fusion.36 = (bf16[16,4,128]{2,1,0:T(4,128)(2,1)}, bf16[16,4,128]{2,1,0:T(4,128)(2,1)}) fusion(bf16[16,16,128]{2,1,0:T(8,128)(2,1)} %param.28), kind=kLoop, calls=%fused_computation.65 | loop fusion | bytes 65536 | tf_op jit(solution)/shard_map/slice | solution.py:12
  9.5 3.0 %collective-permute-start = (bf16[16,4,128]{2,1,0:T(4,128)(2,1)}, bf16[16,4,128]{2,1,0:T(4,128)(2,1)}, u32[]{:S(2)}, u32[]{:S(2)}) collective-permute-start(bf16[16,4,128]{2,1,0:T(4,128)(2,1)} %get-tuple-element.143), channel_id=1, source_target_pairs={{0,4},{4,8},{8,12},{12,0},{1,5},{5,9},{9,13},{13,1},{2,6},{6,10},{... | collective-permute-start | bytes 49160 | tf_op jit(solution)/shard_map/ppermute | solution.py:15
  12.5 2.0 %collective-permute-start.1 = (bf16[16,4,128]{2,1,0:T(4,128)(2,1)}, bf16[16,4,128]{2,1,0:T(4,128)(2,1)}, u32[]{:S(2)}, u32[]{:S(2)}) collective-permute-start(bf16[16,4,128]{2,1,0:T(4,128)(2,1)} %get-tuple-element.144), channel_id=1, source_target_pairs={{4,0},{8,4},{12,8},{0,12},{5,1},{9,5},{13,9},{1,13},{6,2},{10,6},{... | collective-permute-start | bytes 49160 | tf_op jit(solution)/shard_map/ppermute | solution.py:17
  14.6 1.4 copy.18
  16.0 0.7 compare_convert_fusion
  16.7 0.8 multiply_convert_fusion
  17.5 1.3 convert_bitcast_fusion
  18.8 3.3 %copy.19 = bf16[16,16,9,7,24]{4,3,2,1,0:T(8,128)(2,1)} copy(bf16[16,16,9,7,24]{4,0,3,2,1:T(8,128)(2,1)S(1)} %convert_bitcast_fusion) | data formatting | bytes 1548288 | tf_op jit(solution)/shard_map/convert_element_type | solution.py:66
  22.2 0.0 copy-start.3
  22.2 5.5 %reshape_reshape.7 = bf16[16,144,168]{2,1,0:T(8,128)(2,1)S(1)} reshape(bf16[16,16,9,7,24]{4,3,2,1,0:T(8,128)(2,1)} %copy.19) | data formatting | bytes 1548288 | tf_op jit(solution)/shard_map/reshape;reshape | solution.py:74
  27.7 0.0 copy-done.3
  27.7 1.9 %all_gather.3 = bf16[16,16,256]{2,1,0:T(8,128)(2,1)S(1)} all-gather(bf16[16,16,128]{2,1,0:T(8,128)(2,1)S(1)} %copy-done.3), channel_id=1, replica_groups=mesh['ens'=2,'lon'=4,'lat'=2,'ch'=2] {'ch'}, dimensions={2}, use_global_device_ids=true | all-gather | bytes 196608 | tf_op jit(solution)/shard_map/all_gather | solution.py:87
  29.6 0.0 copy-done
  29.6 0.4 convolution_convert_fusion
  30.0 0.2 copy.21
  30.2 0.7 fusion.1
  30.9 0.0 copy-start.2
  31.2 0.0 collective-permute-done
  31.2 0.0 collective-permute-done.1
  31.2 0.6 copy-done.2
  31.8 0.8 pad_maximum_fusion.1
  32.6 3.6 %collective-permute-start.2 = (bf16[3,24,128]{2,1,0:T(8,128)(2,1)S(1)}, bf16[3,24,128]{2,1,0:T(8,128)(2,1)S(1)}, u32[]{:S(2)}, u32[]{:S(2)}) collective-permute-start(bf16[3,24,128]{2,1,0:T(8,128)(2,1)S(1)} %get-tuple-element.142), channel_id=1, source_target_pairs={{0,2},{1,3},{4,6},{5,7},{8,10},{9,11},{12,14},{13,15},{16,18},{17,... | collective-permute-start | bytes 55304 | tf_op jit(solution)/shard_map/ppermute | solution.py:15
  36.2 1.3 collective-permute-start.3
  37.6 0.1 collective-permute-done.2
  37.6 4.2 %collective-permute-done.3 = bf16[3,24,128]{2,1,0:T(8,128)(2,1)S(1)} collective-permute-done((bf16[3,24,128]{2,1,0:T(8,128)(2,1)S(1)}, bf16[3,24,128]{2,1,0:T(8,128)(2,1)S(1)}, u32[]{:S(2)}, u32[]{:S(2)}) %collective-permute-start.3) | collective-permute-done | bytes 18464 | tf_op jit(solution)/shard_map/ppermute | solution.py:17
  41.9 0.9 pad_maximum_fusion
  42.8 0.8 bitcast_dynamic-update-slice_fusion
  43.7 0.1 copy.20
  43.8 1.3 convolution_convert_fusion.1
  45.0 1.8 %dot_general.22 = bf16[16,16,1152]{2,1,0:T(8,128)(2,1)S(1)} reshape(bf16[16,144,128]{2,1,0:T(8,128)(2,1)} %convolution_convert_fusion.1) | data formatting | bytes 1179648 | tf_op jit(solution)/shard_map/dot_general | solution.py:81
  46.9 0.0 copy-start.1
  46.9 1.0 fusion.37
  47.9 0.0 reduce-scatter.2.cloned.1.call-update
  47.9 0.0 all-reduce.4.cloned.1.call-start
  48.1 1.9 %collective-permute-start.4 = (bf16[22,4,128]{2,1,0:T(4,128)(2,1)S(1)}, bf16[22,4,128]{2,1,0:T(4,128)(2,1)S(1)}, u32[]{:S(2)}, u32[]{:S(2)}) collective-permute-start(bf16[22,4,128]{2,1,0:T(4,128)(2,1)S(1)} %get-tuple-element.138), channel_id=1, source_target_pairs={{0,12},{4,0},{8,4},{12,8},{1,13},{5,1},{9,5},{13,9},{2,14},{6,2},{... | collective-permute-start | bytes 67592 | tf_op jit(solution)/shard_map/ppermute | solution.py:27
  50.0 0.0 copy-done.1
  50.0 0.7 reshape_reshape.8
  50.7 1.4 fusion.38
  52.0 0.0 all-reduce.4.cloned.1.call-update
  52.1 0.3 collective-permute-start.5
  52.4 0.0 collective-permute-done.4
  52.4 5.3 %collective-permute-done.5 = bf16[22,4,128]{2,1,0:T(4,128)(2,1)S(1)} collective-permute-done((bf16[22,4,128]{2,1,0:T(4,128)(2,1)S(1)}, bf16[22,4,128]{2,1,0:T(4,128)(2,1)S(1)}, u32[]{:S(2)}, u32[]{:S(2)}) %collective-permute-start.5) | collective-permute-done | bytes 22560 | tf_op jit(solution)/shard_map/ppermute | solution.py:27
  57.8 1.3 collective-permute-start.6
  59.1 4.5 %collective-permute-start.7 = (f32[3,16,128]{2,1,0:T(8,128)S(1)}, f32[3,16,128]{2,1,0:T(8,128)S(1)}, u32[]{:S(2)}, u32[]{:S(2)}) collective-permute-start(f32[3,16,128]{2,1,0:T(8,128)S(1)} %get-tuple-element.135), channel_id=1, source_target_pairs={{0,2},{1,3},{4,6},{5,7},{8,10},{9,11},{12,14},{13,15},{16,18},{17,... | collective-permute-start | bytes 73736 | tf_op jit(solution)/shard_map/ppermute | solution.py:33
  63.6 0.0 collective-permute-done.6
  63.7 1.5 %collective-permute-done.7 = f32[3,16,128]{2,1,0:T(8,128)S(1)} collective-permute-done((f32[3,16,128]{2,1,0:T(8,128)S(1)}, f32[3,16,128]{2,1,0:T(8,128)S(1)}, u32[]{:S(2)}, u32[]{:S(2)}) %collective-permute-start.7) | collective-permute-done | bytes 24608 | tf_op jit(solution)/shard_map/ppermute | solution.py:33
  65.1 0.6 convert_element_type.53
  65.8 0.0 reduce-scatter.2.cloned.1.call-done
  65.8 1.5 %convert_element_type.49 = bf16[16,16,128]{2,1,0:T(8,128)(2,1)} convert(f32[16,16,128]{2,1,0:T(8,128)} %reduce-scatter.2.cloned.1.call-done) | non-fusion elementwise | flops 32768 | bytes 196608 | tf_op jit(solution)/shard_map/convert_element_type | solution.py:84
  67.3 63.7 %all-reduce.4.cloned.1.call-done = f32[9,128,256]{2,1,0:T(8,128)} async-done(((f32[9,128,256]{2,1,0:T(8,128)}), f32[9,128,256]{2,1,0:T(8,128)}) %all-reduce.4.cloned.1.call-update) | async-done | bytes 1179664 | tf_op jit(solution)/shard_map/psum | solution.py:92
  131.0 2.4 %copy.58 = f32[9,128,256]{2,1,0:T(8,128)} copy(f32[9,128,256]{2,1,0:T(8,128)} %all-reduce.4.cloned.1.call-done) | data formatting | bytes 2359296
  (27 shorter events, 0.6 us)
Async XLA Ops:
  8.0 21.7 %copy-start = (bf16[9,128,256]{2,1,0:T(8,128)(2,1)S(1)}, bf16[9,128,256]{2,1,0:T(8,128)(2,1)}, u32[]{:S(2)}) copy-start(bf16[9,128,256]{2,1,0:T(8,128)(2,1)} %param.32) | copy-start | bytes 1769476
  8.0 57.8 %reduce-scatter.2.cloned.1.call-start = ((), (), s32[]{:S(2)}) async-start(), calls=%async_computation.1 | async-start | bytes 393216 | tf_op jit(solution)/shard_map/reduce_scatter | solution.py:84
  9.5 21.7 %collective-permute-start = (bf16[16,4,128]{2,1,0:T(4,128)(2,1)}, bf16[16,4,128]{2,1,0:T(4,128)(2,1)}, u32[]{:S(2)}, u32[]{:S(2)}) collective-permute-start(bf16[16,4,128]{2,1,0:T(4,128)(2,1)} %get-tuple-element.143), channel_id=1, source_target_pairs={{0,4},{4,8},{8,12},{12,0},{1,5},{5,9},{9,13},{13,1},{2,6},{6,10},{... | collective-permute-start | bytes 49160 | tf_op jit(solution)/shard_map/ppermute | solution.py:15
  12.5 18.7 %collective-permute-start.1 = (bf16[16,4,128]{2,1,0:T(4,128)(2,1)}, bf16[16,4,128]{2,1,0:T(4,128)(2,1)}, u32[]{:S(2)}, u32[]{:S(2)}) collective-permute-start(bf16[16,4,128]{2,1,0:T(4,128)(2,1)} %get-tuple-element.144), channel_id=1, source_target_pairs={{4,0},{8,4},{12,8},{0,12},{5,1},{9,5},{13,9},{1,13},{6,2},{10,6},{... | collective-permute-start | bytes 49160 | tf_op jit(solution)/shard_map/ppermute | solution.py:17
  22.2 5.6 %copy-start.3 = (bf16[16,16,128]{2,1,0:T(8,128)(2,1)S(1)}, bf16[16,16,128]{2,1,0:T(8,128)(2,1)}, u32[]{:S(2)}) copy-start(bf16[16,16,128]{2,1,0:T(8,128)(2,1)} %param.33) | copy-start | bytes 196612
  30.9 0.8 copy-start.2
  32.6 5.1 %collective-permute-start.2 = (bf16[3,24,128]{2,1,0:T(8,128)(2,1)S(1)}, bf16[3,24,128]{2,1,0:T(8,128)(2,1)S(1)}, u32[]{:S(2)}, u32[]{:S(2)}) collective-permute-start(bf16[3,24,128]{2,1,0:T(8,128)(2,1)S(1)} %get-tuple-element.142), channel_id=1, source_target_pairs={{0,2},{1,3},{4,6},{5,7},{8,10},{9,11},{12,14},{13,15},{16,18},{17,... | collective-permute-start | bytes 55304 | tf_op jit(solution)/shard_map/ppermute | solution.py:15
  36.2 5.7 %collective-permute-start.3 = (bf16[3,24,128]{2,1,0:T(8,128)(2,1)S(1)}, bf16[3,24,128]{2,1,0:T(8,128)(2,1)S(1)}, u32[]{:S(2)}, u32[]{:S(2)}) collective-permute-start(bf16[3,24,128]{2,1,0:T(8,128)(2,1)S(1)} %get-tuple-element.141), channel_id=1, source_target_pairs={{2,0},{3,1},{6,4},{7,5},{10,8},{11,9},{14,12},{15,13},{18,16},{19,... | collective-permute-start | bytes 55304 | tf_op jit(solution)/shard_map/ppermute | solution.py:17
  46.9 3.1 %copy-start.1 = (bf16[16,144,128]{2,1,0:T(8,128)(2,1)S(1)}, bf16[16,144,128]{2,1,0:T(8,128)(2,1)}, u32[]{:S(2)}) copy-start(bf16[16,144,128]{2,1,0:T(8,128)(2,1)} %convolution_convert_fusion.1) | copy-start | bytes 1769476
  47.9 83.1 %all-reduce.4.cloned.1.call-start = ((), (), s32[]{:S(2)}) async-start(), calls=%async_computation.2 | async-start | bytes 2359296 | tf_op jit(solution)/shard_map/psum | solution.py:92
  48.1 4.3 %collective-permute-start.4 = (bf16[22,4,128]{2,1,0:T(4,128)(2,1)S(1)}, bf16[22,4,128]{2,1,0:T(4,128)(2,1)S(1)}, u32[]{:S(2)}, u32[]{:S(2)}) collective-permute-start(bf16[22,4,128]{2,1,0:T(4,128)(2,1)S(1)} %get-tuple-element.138), channel_id=1, source_target_pairs={{0,12},{4,0},{8,4},{12,8},{1,13},{5,1},{9,5},{13,9},{2,14},{6,2},{... | collective-permute-start | bytes 67592 | tf_op jit(solution)/shard_map/ppermute | solution.py:27
  52.1 5.7 %collective-permute-start.5 = (bf16[22,4,128]{2,1,0:T(4,128)(2,1)S(1)}, bf16[22,4,128]{2,1,0:T(4,128)(2,1)S(1)}, u32[]{:S(2)}, u32[]{:S(2)}) collective-permute-start(bf16[22,4,128]{2,1,0:T(4,128)(2,1)S(1)} %get-tuple-element.137), channel_id=1, source_target_pairs={{0,4},{4,8},{8,12},{12,0},{1,5},{5,9},{9,13},{13,1},{2,6},{6,10},{... | collective-permute-start | bytes 67592 | tf_op jit(solution)/shard_map/ppermute | solution.py:27
  57.8 5.9 %collective-permute-start.6 = (f32[3,16,128]{2,1,0:T(8,128)S(1)}, f32[3,16,128]{2,1,0:T(8,128)S(1)}, u32[]{:S(2)}, u32[]{:S(2)}) collective-permute-start(f32[3,16,128]{2,1,0:T(8,128)S(1)} %get-tuple-element.136), channel_id=1, source_target_pairs={{2,0},{3,1},{6,4},{7,5},{10,8},{11,9},{14,12},{15,13},{18,16},{19,... | collective-permute-start | bytes 73736 | tf_op jit(solution)/shard_map/ppermute | solution.py:33
  59.1 6.1 %collective-permute-start.7 = (f32[3,16,128]{2,1,0:T(8,128)S(1)}, f32[3,16,128]{2,1,0:T(8,128)S(1)}, u32[]{:S(2)}, u32[]{:S(2)}) collective-permute-start(f32[3,16,128]{2,1,0:T(8,128)S(1)} %get-tuple-element.135), channel_id=1, source_target_pairs={{0,2},{1,3},{4,6},{5,7},{8,10},{9,11},{12,14},{13,15},{16,18},{17,... | collective-permute-start | bytes 73736 | tf_op jit(solution)/shard_map/ppermute | solution.py:33
Sparse Core Ops, SparseCore 0:
  48.1 6.1 reduce-scatter.1
Sparse Core Ops, SparseCore 1:
  52.9 78.1 all-reduce.3
where the time goes:
time: 142 us; the launch traced here: 141 us
  waiting for transfers between devices  74.9 us (53%)
  starting transfers between devices  18 us (13%)
  local copies, waits for them, and re-layouts  17.6 us (12%)
  between operations  15.8 us (11%)
  other arithmetic  6.54 us (5%)
  matrix products  6.09 us (4%)
  blocking collectives  1.9 us (1%)
    psum x1, waiting for transfers between devices, body(): lax.psum(grad_local, ('lon', 'lat')).reshape(kernels, channels, out_width)  63.7 us
    ppermute x2, starting transfers between devices, with_halo(): lax.ppermute(tail, axis, [(i, (i + 1) % count) for i in range(ends)])  6.64 us
    ppermute x2, starting transfers between devices, shifted(): lax.ppermute(value, axis, [(source, source + steps) for source in range(i...  5.84 us
    another operation x1, local copies, waits for them, and re-layouts, body(): tiles.reshape(lat_rows, lon_cols * kernels, lat_span * ext_width)  5.55 us
    ppermute x2, waiting for transfers between devices, passed_along(): return lax.ppermute(value, axis, pairs)  5.31 us
    unnamed x15, local copies, waits for them, and re-layouts  4.45 us
    ppermute x2, waiting for transfers between devices, with_halo(): lax.ppermute(head, axis, [((i + 1) % count, i) for i in range(ends)])  4.21 us
    convert_element_type x1, local copies, waits for them, and re-layouts, body(): tiles.astype(jnp.bfloat16)  3.34 us
  transfers between devices with their start and end apart: 10, of which 5 were waited for; matrix products, arithmetic and copies ran while one was open for 14% of the time, Pallas kernels for 0%

commit v1 on v0

v1 whole, which is shorter than its diff:
```python
import functools

import jax
import jax.numpy as jnp
from jax import lax
from jax.experimental import pallas as pl
from jax.experimental.pallas import tpu as pltpu
from jax.sharding import PartitionSpec as P

MESH = pl.DeviceIdType.MESH
QS = 32
BF = jnp.bfloat16
F32 = jnp.float32


def dot(a, b, ca, cb):
    return lax.dot_general(a, b, (((ca,), (cb,)), ((), ())), preferred_element_type=F32)


def kernel(
    dims,
    feat,
    base,
    weight,
    cot,
    out,
    igrad,
    wg,
    ext,
    acc,
    tiles,
    mixed,
    spread,
    cotf,
    pout,
    pin,
    fpk,
    edge,
    ein,
    ecorn,
    elat,
    gpk,
    gedge,
    gin,
    gcorn,
    glat,
    gf,
    gb,
    rx,
    zb,
    rz,
    zown,
    s_ch,
    r_ch,
    s_f,
    r_f,
    s_g,
    r_g,
    s_rx,
    r_rx,
    s_rz,
    r_rz,
    s_az,
    r_az,
    s_ax,
    r_ax,
):
    L, N, half, lon_half, per_lat, pc = dims
    R, J, C = feat.shape
    K = weight.shape[0]
    cells = R * J
    ens, n, l, ch = (lax.axis_index(a) for a in ("ens", "lon", "lat", "ch"))
    left, right = lax.rem(n + N - 1, N), lax.rem(n + 1, N)
    has_up, has_down = l > 0, l < L - 1

    def dev(lat, lon):
        return (ens, lon, lat, ch)

    mate = (ens, n, l, 1 - ch)
    lats = [lax.rem(l + d, L) for d in range(1, L)]
    lons = [lax.rem(n + d, N) for d in range(1, N)]

    def remote(src, dst, ss, rs, device):
        return pltpu.make_async_remote_copy(
            src_ref=src, dst_ref=dst, send_sem=ss, recv_sem=rs, device_id=device, device_id_type=MESH
        )

    barrier = pltpu.get_barrier_semaphore()

    def greet(device):
        pl.semaphore_signal(barrier, inc=1, device_id=device, device_id_type=MESH)

    greet(mate)
    for lat in lats:
        greet(dev(lat, n))
    for lon in lons:
        greet(dev(l, lon))
    for has, lat in ((has_up, l - 1), (has_down, l + 1)):

        @pl.when(has)
        def _():
            greet(dev(lat, left))
            greet(dev(lat, right))

    for r in range(R):
        row = feat[r].astype(F32)
        fpk[0, 4 * r : 4 * r + 4] = row[:lon_half]
        fpk[1, 4 * r : 4 * r + 4] = row[J - lon_half :]
    edge[...] = fpk[...].astype(BF)

    corners = 2 * (has_up.astype(jnp.int32) + has_down.astype(jnp.int32))
    pl.semaphore_wait(barrier, 1 + (L - 1) + (N - 1) + corners)

    def edge_copies(src, dst, corn_src, corn_dst, lat_src, lat_dst, ss, rs):
        def lon_copy(side):
            return remote(src(side), dst(1 - side), ss.at[side], rs.at[1 - side], dev(l, (left, right)[side]))

        def corner(side, down):
            lat = l + 1 if down else l - 1
            return remote(
                corn_src(side, down),
                corn_dst(1 - side, 1 - down),
                ss.at[2 + 2 * side + down],
                rs.at[2 + 2 * (1 - side) + (1 - down)],
                dev(lat, (left, right)[side]),
            )

        def lat_copy(down):
            lat = l + 1 if down else l - 1
            return remote(lat_src(down), lat_dst(1 - down), ss.at[6 + down], rs.at[6 + 1 - down], dev(lat, n))

        return lon_copy, corner, lat_copy

    def each(copies, action):
        lon_copy, corner, lat_copy = copies
        for side in (0, 1):
            action(lon_copy(side))
        for down, has in ((0, has_up), (1, has_down)):

            @pl.when(has)
            def _():
                action(lat_copy(down))
                for side in (0, 1):
                    action(corner(side, down))

    fwd = edge_copies(
        lambda s: edge.at[s],
        lambda s: ein.at[s],
        lambda s, d: edge.at[s, pl.ds(48 if d else 0, 16)],
        lambda s, d: ecorn.at[2 * s + d],
        lambda d: feat.at[pl.ds(R - half if d else 0, half)],
        lambda d: elat.at[d],
        s_f,
        r_f,
    )
    cot_copy = remote(cot, cotf.at[ch], s_ch.at[0], r_ch.at[0], mate)
    each(fwd, lambda c: c.start())
    cot_copy.start()

    cotf[ch] = cot[...]
    ext[...] = jnp.zeros_like(ext)
    acc[...] = jnp.zeros_like(acc)

    def make_tiles(i, _):
        for k in range(K):
            line = base[k, pl.ds(i, 1), :]
            for h in range(2):
                flat = jnp.broadcast_to(line[:, 128 * h : 128 * h + 128], (J, 128))
                turned = pltpu.roll(flat, 8 - lon_half, 1, stride=1, stride_axis=0)
                tiles[i, J * k : J * k + J, 128 * h : 128 * h + 128] = turned.astype(BF)
        return _

    lax.fori_loop(0, R, make_tiles, 0)

    for r in range(R):
        ext[r + half, 8 : 8 + J] = feat[r].astype(F32)

    def recv_wait(dst, sem):
        remote(dst, dst, sem, sem, mate).wait_recv()

    for side in (0, 1):
        recv_wait(ein.at[side], r_f.at[side])
        cols = ein[side].astype(F32)
        at = 8 - lon_half if side == 0 else 8 + J
        for r in range(R):
            ext[r + half, at : at + lon_half] = cols[4 * r : 4 * r + 4]
    for down, has in ((0, has_up), (1, has_down)):
        first = half + R if down else 0

        @pl.when(has)
        def _():
            recv_wait(elat.at[down], r_f.at[6 + down])
            for r in range(half):
                ext[first + r, 8 : 8 + J] = elat[down, r].astype(F32)
            for side in (0, 1):
                recv_wait(ecorn.at[2 * side + down], r_f.at[2 + 2 * side + down])
                cols = ecorn[2 * side + down].astype(F32)
                at = 8 - lon_half if side == 0 else 8 + J
                skip = 0 if down else 4
                for r in range(half):
                    ext[first + r, at : at + lon_half] = cols[skip + 4 * r : skip + 4 * r + 4]

    def mix(i, _):
        window = ext[pl.ds(i, 8)].reshape(8 * QS, C).astype(BF)
        row = dot(tiles[i], window, 1, 0).astype(BF)
        for k in range(K):
            mixed[k, pl.ds(pl.multiple_of(i * J, J), J)] = row[J * k : J * k + J]
        return _

    lax.fori_loop(0, R, mix, 0)

    cot_copy.wait_recv()
    cot_full = jnp.concatenate(
        [cotf[0].reshape(cells, C), cotf[1].reshape(cells, C)], axis=1
    )

    for k in range(K):
        g = dot(mixed[k], cot_full, 0, 0)
        gf[C * k : C * k + C] = g
        gb[C * k : C * k + C] = g.astype(BF)

    def rows(lat, c):
        start = lat * per_lat + jnp.minimum(c * pc, per_lat - pc)
        return pl.ds(pl.multiple_of(start, 16), pc)

    order = lons + [n]

    def rx_copy(lat, c):
        return remote(gb.at[rows(lat, c)], rx.at[l, c], s_rx.at[lat, c], r_rx.at[l, c], dev(lat, n))

    for c in order:
        for lat in lats:
            rx_copy(lat, c).start()

    def rz_copy(c):
        return remote(zb.at[c], rz.at[n], s_rz.at[c], r_rz.at[n], dev(l, c))

    def lat_sum(c):
        total = gf[rows(l, c)]
        for lat in lats:
            recv_wait(rx.at[lat, c], r_rx.at[lat, c])
            total = total + rx[lat, c].astype(F32)
        return total

    def pass_on(c):
        zb[c] = lat_sum(c).astype(BF)
        rz_copy(c).start()

    passes = list(order[:-1])

    total = dot(mixed[0], weight[0], 1, 0)
    for k in range(1, K):
        total = total + dot(mixed[k], weight[k], 1, 0)
    pout[0] = total[:, :C]
    pout[1] = total[:, C:]
    out_copy = remote(pout.at[1 - ch], pin, s_ch.at[1], r_ch.at[1], mate)
    out_copy.start()
    pass_on(passes[0])

    for k in range(K):
        part = dot(cot_full, weight[k], 1, 1).astype(BF)
        spread[:, J * k : J * k + J] = part.reshape(R, J, C)
    for c in passes[1:2]:
        pass_on(c)

    def back(i, _):
        part = dot(tiles[i], spread[i], 0, 0)
        acc[pl.ds(i, 8)] += part.reshape(8, QS, C)
        return _

    lax.fori_loop(0, R // 2, back, 0)
    for c in passes[2:3]:
        pass_on(c)
    lax.fori_loop(R // 2, R, back, 0)
    for c in passes[3:]:
        pass_on(c)
    zown[...] = lat_sum(n)

    gpk[...] = jnp.zeros_like(gpk)
    for side in (0, 1):
        at = 8 - lon_half if side == 0 else 8 + J
        for r in range(R):
            gpk[side, 4 * r : 4 * r + 4] = acc[r + half, at : at + lon_half]
        for r in range(half):
            gpk[side, 64 + 4 * r : 68 + 4 * r] = acc[r, at : at + lon_half]
            gpk[side, 80 + 4 * r : 84 + 4 * r] = acc[R + half + r, at : at + lon_half]
    gedge[...] = gpk[...].astype(BF)
    bwd = edge_copies(
        lambda s: gedge.at[s, pl.ds(0, 64)],
        lambda s: gin.at[s],
        lambda s, d: gedge.at[s, pl.ds(80 if d else 64, 16)],
        lambda s, d: gcorn.at[2 * s + d],
        lambda d: acc.at[pl.ds(R + half if d else 0, half), pl.ds(8, J)],
        lambda d: glat.at[d],
        s_g,
        r_g,
    )
    each(bwd, lambda c: c.start())

    total = zown[...]
    for c in lons:
        recv_wait(rz.at[c], r_rz.at[c])
        total = total + rz[c].astype(F32)
    wg[l, n] = total.astype(BF)

    def az_copy(lon):
        return remote(wg.at[l, n], wg.at[l, n], s_az.at[lon], r_az.at[n], dev(l, lon))

    def ax_copy(lat, c):
        return remote(wg.at[l, c], wg.at[l, c], s_ax.at[lat, c], r_ax.at[l, c], dev(lat, n))

    for lon in lons:
        az_copy(lon).start()
    for lat in lats:
        ax_copy(lat, n).start()

    out_copy.wait_recv()
    out[...] = (pout[ch] + pin[...]).astype(BF).reshape(R, J, C)

    for side in (0, 1):
        recv_wait(gin.at[side], r_g.at[side])
        cols = gin[side].astype(F32)
        at = 8 if side == 0 else 8 + J - lon_half
        for r in range(R):
            acc[r + half, at : at + lon_half] += cols[4 * r : 4 * r + 4]
    for down, has in ((0, has_up), (1, has_down)):
        first = R if down else half

        @pl.when(has)
        def _():
            recv_wait(glat.at[down], r_g.at[6 + down])
            for r in range(half):
                acc[first + r, 8 : 8 + J] += glat[down, r]
            for side in (0, 1):
                recv_wait(gcorn.at[2 * side + down], r_g.at[2 + 2 * side + down])
                cols = gcorn[2 * side + down].astype(F32)
                at = 8 if side == 0 else 8 + J - lon_half
                for r in range(half):
                    acc[first + r, at : at + lon_half] += cols[4 * r : 4 * r + 4]
    for r in range(R):
        igrad[r] = acc[r + half, 8 : 8 + J].astype(BF)

    for c in lons:
        recv_wait(wg.at[l, c], r_az.at[c])
        for lat in lats:
            ax_copy(lat, c).start()
    for c in [n] + lons:
        for lat in lats:
            recv_wait(wg.at[lat, c], r_ax.at[lat, c])

    cot_copy.wait_send()
    out_copy.wait_send()
    each(fwd, lambda c: c.wait_send())
    each(bwd, lambda c: c.wait_send())
    for c in lons:
        rz_copy(c).wait_send()
        az_copy(c).wait_send()
    for c in order:
        for lat in lats:
            rx_copy(lat, c).wait_send()
            ax_copy(lat, c).wait_send()


def live_basis(basis, active, reach, lon_half):
    distance = jnp.abs(jnp.arange(2 * lon_half + 1, dtype=jnp.int32) - lon_half)
    lon_live = (distance[None, :] <= reach[:, None]).astype(jnp.int32)
    live_mask = active[:, :, None] * lon_live[:, None, :]
    return basis * live_mask[None].astype(basis.dtype)


def body(features, basis, active, reach, weight, cotangent):
    R, J, C = features.shape
    K, _, lat_span, lon_span = basis.shape
    half, lon_half = (lat_span - 1) // 2, (lon_span - 1) // 2
    O = weight.shape[2]
    L, N = lax.axis_size("lat"), lax.axis_size("lon")
    per_lat = K * C // L
    pc = -(-per_lat // (16 * N)) * 16
    cells = R * J

    first = lax.axis_index("lat") * R
    own = lax.dynamic_slice_in_dim(basis, first, R, 1)
    own = live_basis(
        own,
        lax.dynamic_slice_in_dim(active, first, R, 0),
        lax.dynamic_slice_in_dim(reach, first, R, 0),
        lon_half,
    ).astype(F32)
    base = jnp.pad(own, ((0, 0), (0, 0), (0, 8 - lat_span), (0, QS - lon_span)))
    base = base.reshape(K, R, 8 * QS)

    vmem = pl.BlockSpec(memory_space=pltpu.VMEM)
    dma = pltpu.SemaphoreType.DMA
    output, input_grad, wg = pl.pallas_call(
        functools.partial(kernel, (L, N, half, lon_half, per_lat, pc)),
        out_shape=(
            jax.ShapeDtypeStruct((R, J, C), BF),
            jax.ShapeDtypeStruct((R, J, C), BF),
            jax.ShapeDtypeStruct((L, N, pc, O), BF),
        ),
        in_specs=[vmem] * 4,
        out_specs=(vmem,) * 3,
        scratch_shapes=[
            pltpu.VMEM((R + 8, QS, C), F32),
            pltpu.VMEM((R + 8, QS, C), F32),
            pltpu.VMEM((R, K * J, 8 * QS), BF),
            pltpu.VMEM((K, cells, C), BF),
            pltpu.VMEM((R, K * J, C), BF),
            pltpu.VMEM((2, R, J, C), BF),
            pltpu.VMEM((2, cells, C), F32),
            pltpu.VMEM((cells, C), F32),
            pltpu.VMEM((2, 64, C), F32),
            pltpu.VMEM((2, 64, C), BF),
            pltpu.VMEM((2, 64, C), BF),
            pltpu.VMEM((4, 16, C), BF),
            pltpu.VMEM((2, half, J, C), BF),
            pltpu.VMEM((2, 96, C), F32),
            pltpu.VMEM((2, 96, C), BF),
            pltpu.VMEM((2, 64, C), BF),
            pltpu.VMEM((4, 16, C), BF),
            pltpu.VMEM((2, half, J, C), F32),
            pltpu.VMEM((K * C, O), F32),
            pltpu.VMEM((K * C, O), BF),
            pltpu.VMEM((L, N, pc, O), BF),
            pltpu.VMEM((N, pc, O), BF),
            pltpu.VMEM((N, pc, O), BF),
            pltpu.VMEM((pc, O), F32),
            dma((2,)),
            dma((2,)),
            dma((8,)),
            dma((8,)),
            dma((8,)),
            dma((8,)),
            dma((L, N)),
            dma((L, N)),
            dma((N,)),
            dma((N,)),
            dma((N,)),
            dma((N,)),
            dma((L, N)),
            dma((L, N)),
        ],
        compiler_params=pltpu.CompilerParams(
            collective_id=0, has_side_effects=True, vmem_limit_bytes=40 * 1024 * 1024
        ),
    )(features, base, weight, cotangent)
    weight_grad = wg.reshape(L, N * pc, O)[:, :per_lat].reshape(K, C, O).astype(F32)
    return output, input_grad, weight_grad


def solution(mesh):
    return jax.shard_map(
        body,
        mesh=mesh,
        in_specs=(
            P(("ens", "lat"), "lon", "ch"),
            P(),
            P(),
            P(),
            P(None, "ch", None),
            P(("ens", "lat"), "lon", "ch"),
        ),
        out_specs=(
            P(("ens", "lat"), "lon", "ch"),
            P(("ens", "lat"), "lon", "ch"),
            P("ens", "ch", None),
        ),
        check_vma=False,
    )
```

time: 142 us -> 41.3 us (0.29)
  waiting for transfers between devices: 74.9 us -> 0 us
  Pallas kernels: 0 us -> 34.6 us
  starting transfers between devices: 18 us -> 0 us
  between operations: 15.8 us -> 0.73 us
  local copies, waits for them, and re-layouts: 17.6 us -> 4.46 us
  matrix products: 6.09 us -> 0 us
  other arithmetic: 6.54 us -> 1.37 us
  blocking collectives: 1.9 us -> 0 us
    psum x1 -> x0, waiting for transfers between devices: 63.7 us -> none  [body(): lax.psum(grad_local, ('lon', 'lat')).reshape(kernels, channels, out_width)]
    pallas_call x0 -> x1, Pallas kernels: none -> 34.6 us  [body(): pl.pallas_call(functools.partial(kernel, (L, N, half, lon_half, per_lat,...]
    ppermute x8 -> x0, starting transfers between devices: 17.9 us -> none  [the longest x2 6.64 us: with_halo(): lax.ppermute(tail, axis, [(i, (i + 1) % count) for i in range(ends)])]
    ppermute x8 -> x0, waiting for transfers between devices: 11.1 us -> none  [the longest x2 5.31 us: passed_along(): return lax.ppermute(value, axis, pairs)]
    another operation x4 -> x0, local copies, waits for them, and re-layouts: 6.33 us -> none  [the longest x1 5.55 us: body(): tiles.reshape(lat_rows, lon_cols * kernels, lat_span * ext_width)]
    dot_general x6 -> x0, matrix products: 6.09 us -> none  [the longest x2 2.01 us: body(): lax.dot_general(tiles.reshape(lat_rows, lon_cols * kernels, lat_span * ex...]
    convert_element_type x2 -> x0, local copies, waits for them, and re-layouts: 3.5 us -> none  [the longest x1 3.34 us: body(): tiles.astype(jnp.bfloat16)]
    unnamed x15 -> x11, local copies, waits for them, and re-layouts: 4.45 us -> 2.54 us
  transfers between devices with their start and end apart: 10 -> 0, of which waited for: 5 -> 0; matrix products, arithmetic and copies ran while one was open for 14% -> 0% of each run, Pallas kernels for 0% -> 0%
where the time goes in v1:
time: 41.3 us; the launch traced here: 41.1 us
  Pallas kernels  34.6 us (84%)
  local copies, waits for them, and re-layouts  4.46 us (11%)
  other arithmetic  1.37 us (3%)
  between operations  0.73 us (2%)
    pallas_call x1, Pallas kernels, body(): pl.pallas_call(functools.partial(kernel, (L, N, half, lon_half, per_lat,...  34.6 us
    unnamed x11, local copies, waits for them, and re-layouts  2.54 us
    convert_element_type x1, other arithmetic, body(): wg.reshape(L, N * pc, O)[:, :per_lat].reshape(K, C, O).astype(F32)  1.13 us
    dynamic_slice x2, local copies, waits for them, and re-layouts, body(): lax.dynamic_slice_in_dim(active, first, R, 0)  0.84 us

profile of v1, /device:TPU:0, one launch (start us, length us, event | category | flops | bytes accessed | tf_op | source)
XLA Modules:
  0.0 41.1 jit_solution(16452701104165479418)
XLA Ops:
  0.6 0.0 copy-start
  0.7 0.8 %dynamic_slice.11 = s32[16]{0:T(128)S(1)} dynamic-slice(s32[32]{0:T(128)} %param.9, s32[]{:T(128)S(6)} %select_n.2), dynamic_slice_sizes={16} | dynamic-slice | bytes 132 | tf_op jit(solution)/shard_map/dynamic_slice | solution.py:386
  1.4 0.8 %constant_dynamic-slice_fusion = s32[16,7]{0,1:T(8,128)S(1)} fusion(s32[32,7]{0,1:T(8,128)} %param.8, s32[]{:T(128)S(6)} %select_n.2), kind=kLoop, calls=%fused_computation.5 | loop fusion | bytes 900 | tf_op jit(solution)/shard_map/dynamic_slice | solution.py:385
  2.2 0.1 copy.11
  2.3 0.1 compare_convert_fusion
  2.3 0.1 multiply_convert_fusion
  2.4 0.0 copy-done
  2.4 0.1 constant_dynamic-slice_fusion.1
  2.6 0.5 %copy.12 = bf16[9,16,7,9]{3,2,1,0:T(8,128)(2,1)S(1)} copy(bf16[9,16,7,9]{1,2,3,0:T(8,128)(2,1)S(1)} %constant_dynamic-slice_fusion.1) | data formatting | bytes 36288
  3.1 0.0 copy-start.1
  3.1 0.0 copy-start.2
  3.1 0.0 copy-start.3
  3.2 0.1 pad_convert_fusion
  3.2 0.2 reshape.49.base
  3.4 0.7 %copy-done.1 = bf16[9,128,256]{2,1,0:T(8,128)(2,1)S(1)} copy-done((bf16[9,128,256]{2,1,0:T(8,128)(2,1)S(1)}, bf16[9,128,256]{2,1,0:T(8,128)(2,1)}, u32[]{:S(2)}) %copy-start.1) | copy-done | bytes 589848
  4.2 0.0 copy-done.2
  4.2 0.0 copy-done.3
  4.2 34.6 %shard_map.85 = (bf16[16,16,128]{2,1,0:T(8,128)(2,1)S(1)}, bf16[16,16,128]{2,1,0:T(8,128)(2,1)S(1)}, bf16[2,4,144,256]{3,2,1,0:T(8,128)(2,1)S(1)}) custom-call(bf16[16,16,128]{2,1,0:T(8,128)(2,1)S(1)} %copy-done.2, f32[9,16,256]{2,1,0:T(8,128)S(1)} %reshape.49.base, bf16[9,128,256]{2,1,0:T(8,128)(2,1)S(1)} %copy-done.1, bf16[16,16,128]{2,1,0:T(8,128)(2,1)S(1)} %copy-done.3), custom_call_target="tpu_custom_call" | custom-call | tf_op jit(solution)/shard_map/pallas_call | solution.py:394
  38.7 1.1 %convert.4 = f32[9,128,256]{2,1,0:T(8,128)} convert(bf16[9,128,256]{2,1,0:T(8,128)(2,1)S(1)} %bitcast.4) | non-fusion elementwise | flops 294912 | bytes 1769472 | tf_op jit(solution)/shard_map/convert_element_type | solution.py:447
  39.9 0.6 %copy.15 = bf16[16,16,128]{2,1,0:T(8,128)(2,1)} copy(bf16[16,16,128]{2,1,0:T(8,128)(2,1)S(1)} %get-tuple-element.12) | data formatting | bytes 131072
  40.5 0.6 %copy.16 = bf16[16,16,128]{2,1,0:T(8,128)(2,1)} copy(bf16[16,16,128]{2,1,0:T(8,128)(2,1)S(1)} %get-tuple-element.13) | data formatting | bytes 131072
  (2 shorter events, 0.0 us)
Async XLA Ops:
  0.6 1.8 %copy-start = (bf16[9,32,7,9]{1,2,3,0:T(8,128)(2,1)S(1)}, bf16[9,32,7,9]{1,2,3,0:T(8,128)(2,1)}, u32[]{:S(2)}) copy-start(bf16[9,32,7,9]{1,2,3,0:T(8,128)(2,1)} %param.7) | copy-start | bytes 108868
  3.1 1.1 %copy-start.1 = (bf16[9,128,256]{2,1,0:T(8,128)(2,1)S(1)}, bf16[9,128,256]{2,1,0:T(8,128)(2,1)}, u32[]{:S(2)}) copy-start(bf16[9,128,256]{2,1,0:T(8,128)(2,1)} %weight.1) | copy-start | bytes 1769476
  3.1 1.1 %copy-start.2 = (bf16[16,16,128]{2,1,0:T(8,128)(2,1)S(1)}, bf16[16,16,128]{2,1,0:T(8,128)(2,1)}, u32[]{:S(2)}) copy-start(bf16[16,16,128]{2,1,0:T(8,128)(2,1)} %feat.1) | copy-start | bytes 196612
  3.1 1.0 %copy-start.3 = (bf16[16,16,128]{2,1,0:T(8,128)(2,1)S(1)}, bf16[16,16,128]{2,1,0:T(8,128)(2,1)}, u32[]{:S(2)}) copy-start(bf16[16,16,128]{2,1,0:T(8,128)(2,1)} %cot.1) | copy-start | bytes 196612

commit v2 on v1

--- a/solution.py
+++ b/solution.py
@@ -20,12 +20,15 @@
 def kernel(
     dims,
     feat,
-    base,
+    basis,
+    active,
+    reach,
     weight,
     cot,
     out,
     igrad,
     wg,
+    base,
     ext,
     acc,
     tiles,
@@ -108,6 +111,38 @@
         fpk[1, 4 * r : 4 * r + 4] = row[J - lon_half :]
     edge[...] = fpk[...].astype(BF)
 
+    A, B = basis.shape[2], basis.shape[1]
+    where = lax.broadcasted_iota(jnp.int32, (8 * B, 8 * QS), 0)
+    lane = lax.broadcasted_iota(jnp.int32, (8 * B, 8 * QS), 1)
+    place = (lane == (where % 8) * QS + where // 8).astype(F32).astype(BF)
+    live = active[...]
+    far = reach[...]
+    blank = jnp.zeros((8 - A, live.shape[1]), F32)
+    lives = [(live * (abs(b - lon_half) <= far).astype(jnp.int32)).astype(F32) for b in range(B)]
+    for k in range(K):
+        planes = []
+        for b in range(B):
+            planes += [basis[k, b].astype(F32) * lives[b], blank]
+        base[k] = dot(jnp.concatenate(planes, axis=0).astype(BF), place, 0, 0)
+
+    def make_tiles(i, _):
+        for k in range(K):
+            line = base[k, pl.ds(l * R + i, 1), :]
+            for h in range(2):
+                flat = jnp.broadcast_to(line[:, 128 * h : 128 * h + 128], (J, 128))
+                turned = pltpu.roll(flat, 8 - lon_half, 1, stride=1, stride_axis=0)
+                tiles[i, J * k : J * k + J, 128 * h : 128 * h + 128] = turned.astype(BF)
+        return _
+
+    lax.fori_loop(0, R, make_tiles, 0, unroll=4)
+
+    cotf[ch] = cot[...]
+    ext[...] = jnp.zeros_like(ext)
+    acc[...] = jnp.zeros_like(acc)
+
+    for r in range(R):
+        ext[r + half, 8 : 8 + J] = feat[r].astype(F32)
+
     corners = 2 * (has_up.astype(jnp.int32) + has_down.astype(jnp.int32))
     pl.semaphore_wait(barrier, 1 + (L - 1) + (N - 1) + corners)
 
@@ -157,26 +192,24 @@
     each(fwd, lambda c: c.start())
     cot_copy.start()
 
-    cotf[ch] = cot[...]
-    ext[...] = jnp.zeros_like(ext)
-    acc[...] = jnp.zeros_like(acc)
-
-    def make_tiles(i, _):
-        for k in range(K):
-            line = base[k, pl.ds(i, 1), :]
-            for h in range(2):
-                flat = jnp.broadcast_to(line[:, 128 * h : 128 * h + 128], (J, 128))
-                turned = pltpu.roll(flat, 8 - lon_half, 1, stride=1, stride_axis=0)
-                tiles[i, J * k : J * k + J, 128 * h : 128 * h + 128] = turned.astype(BF)
-        return _
-
-    lax.fori_loop(0, R, make_tiles, 0)
-
-    for r in range(R):
-        ext[r + half, 8 : 8 + J] = feat[r].astype(F32)
-
     def recv_wait(dst, sem):
         remote(dst, dst, sem, sem, mate).wait_recv()
+
+    cot_copy.wait_recv()
+    cot_full = jnp.concatenate(
+        [cotf[0].reshape(cells, C), cotf[1].reshape(cells, C)], axis=1
+    )
+
+    for k in range(K):
+        part = dot(cot_full, weight[k], 1, 1).astype(BF)
+        spread[:, J * k : J * k + J] = part.reshape(R, J, C)
+
+    def back(i, _):
+        part = dot(tiles[i], spread[i], 0, 0)
+        acc[pl.ds(i, 8)] += part.reshape(8, QS, C)
+        return _
+
+    lax.fori_loop(0, R // 2, back, 0, unroll=4)
 
     for side in (0, 1):
         recv_wait(ein.at[side], r_f.at[side])
@@ -207,12 +240,7 @@
             mixed[k, pl.ds(pl.multiple_of(i * J, J), J)] = row[J * k : J * k + J]
         return _
 
-    lax.fori_loop(0, R, mix, 0)
-
-    cot_copy.wait_recv()
-    cot_full = jnp.concatenate(
-        [cotf[0].reshape(cells, C), cotf[1].reshape(cells, C)], axis=1
-    )
+    lax.fori_loop(0, R, mix, 0, unroll=4)
 
     for k in range(K):
         g = dot(mixed[k], cot_full, 0, 0)
@@ -245,8 +273,6 @@
     def pass_on(c):
         zb[c] = lat_sum(c).astype(BF)
         rz_copy(c).start()
-
-    passes = list(order[:-1])
 
     total = dot(mixed[0], weight[0], 1, 0)
     for k in range(1, K):
@@ -255,26 +281,8 @@
     pout[1] = total[:, C:]
     out_copy = remote(pout.at[1 - ch], pin, s_ch.at[1], r_ch.at[1], mate)
     out_copy.start()
-    pass_on(passes[0])
-
-    for k in range(K):
-        part = dot(cot_full, weight[k], 1, 1).astype(BF)
-        spread[:, J * k : J * k + J] = part.reshape(R, J, C)
-    for c in passes[1:2]:
-        pass_on(c)
-
-    def back(i, _):
-        part = dot(tiles[i], spread[i], 0, 0)
-        acc[pl.ds(i, 8)] += part.reshape(8, QS, C)
-        return _
-
-    lax.fori_loop(0, R // 2, back, 0)
-    for c in passes[2:3]:
-        pass_on(c)
-    lax.fori_loop(R // 2, R, back, 0)
-    for c in passes[3:]:
-        pass_on(c)
-    zown[...] = lat_sum(n)
+
+    lax.fori_loop(R // 2, R, back, 0, unroll=4)
 
     gpk[...] = jnp.zeros_like(gpk)
     for side in (0, 1):
@@ -297,6 +305,10 @@
     )
     each(bwd, lambda c: c.start())
 
+    for c in lons:
+        pass_on(c)
+    zown[...] = lat_sum(n)
+
     total = zown[...]
     for c in lons:
         recv_wait(rz.at[c], r_rz.at[c])
@@ -361,33 +373,15 @@
             ax_copy(lat, c).wait_send()
 
 
-def live_basis(basis, active, reach, lon_half):
-    distance = jnp.abs(jnp.arange(2 * lon_half + 1, dtype=jnp.int32) - lon_half)
-    lon_live = (distance[None, :] <= reach[:, None]).astype(jnp.int32)
-    live_mask = active[:, :, None] * lon_live[:, None, :]
-    return basis * live_mask[None].astype(basis.dtype)
-
-
 def body(features, basis, active, reach, weight, cotangent):
     R, J, C = features.shape
-    K, _, lat_span, lon_span = basis.shape
+    K, rows, lat_span, lon_span = basis.shape
     half, lon_half = (lat_span - 1) // 2, (lon_span - 1) // 2
     O = weight.shape[2]
     L, N = lax.axis_size("lat"), lax.axis_size("lon")
     per_lat = K * C // L
     pc = -(-per_lat // (16 * N)) * 16
     cells = R * J
-
-    first = lax.axis_index("lat") * R
-    own = lax.dynamic_slice_in_dim(basis, first, R, 1)
-    own = live_basis(
-        own,
-        lax.dynamic_slice_in_dim(active, first, R, 0),
-        lax.dynamic_slice_in_dim(reach, first, R, 0),
-        lon_half,
-    ).astype(F32)
-    base = jnp.pad(own, ((0, 0), (0, 0), (0, 8 - lat_span), (0, QS - lon_span)))
-    base = base.reshape(K, R, 8 * QS)
 
     vmem = pl.BlockSpec(memory_space=pltpu.VMEM)
     dma = pltpu.SemaphoreType.DMA
@@ -398,9 +392,10 @@
             jax.ShapeDtypeStruct((R, J, C), BF),
             jax.ShapeDtypeStruct((L, N, pc, O), BF),
         ),
-        in_specs=[vmem] * 4,
+        in_specs=[vmem] * 6,
         out_specs=(vmem,) * 3,
         scratch_shapes=[
+            pltpu.VMEM((K, rows, 8 * QS), F32),
             pltpu.VMEM((R + 8, QS, C), F32),
             pltpu.VMEM((R + 8, QS, C), F32),
             pltpu.VMEM((R, K * J, 8 * QS), BF),
@@ -443,7 +438,14 @@
         compiler_params=pltpu.CompilerParams(
             collective_id=0, has_side_effects=True, vmem_limit_bytes=40 * 1024 * 1024
         ),
-    )(features, base, weight, cotangent)
+    )(
+        features,
+        basis.transpose(0, 3, 2, 1),
+        active.T,
+        reach.reshape(1, -1),
+        weight,
+        cotangent,
+    )
     weight_grad = wg.reshape(L, N * pc, O)[:, :per_lat].reshape(K, C, O).astype(F32)
     return output, input_grad, weight_grad
 

time: 41.3 us -> 41.2 us (level)
  local copies, waits for them, and re-layouts: 4.46 us -> 6.25 us
  Pallas kernels: 34.6 us -> 32.9 us
    unnamed x11 -> x14, local copies, waits for them, and re-layouts: 2.54 us -> 6.25 us
    dynamic_slice x4 -> x0, local copies, waits for them, and re-layouts: 1.72 us -> none  [the longest x2 0.84 us: body(): lax.dynamic_slice_in_dim(active, first, R, 0)]
    pallas_call x1, Pallas kernels: 34.6 us -> 32.9 us  [body(): pl.pallas_call(functools.partial(kernel, (L, N, half, lon_half, per_lat,...]
where the time goes in v2:
time: 41.2 us; the launch traced here: 40.9 us
  Pallas kernels  32.9 us (80%)
  local copies, waits for them, and re-layouts  6.25 us (15%)
  other arithmetic  1.13 us (3%)
  between operations  0.65 us (2%)
    pallas_call x1, Pallas kernels, body(): pl.pallas_call(functools.partial(kernel, (L, N, half, lon_half, per_lat,...  32.9 us
    unnamed x14, local copies, waits for them, and re-layouts  6.25 us
    convert_element_type x1, other arithmetic, body(): wg.reshape(L, N * pc, O)[:, :per_lat].reshape(K, C, O).astype(F32)  1.13 us

profile of v2, /device:TPU:0, one launch (start us, length us, event | category | flops | bytes accessed | tf_op | source)
XLA Modules:
  0.0 40.9 jit_solution(3241207198341649694)
XLA Ops:
  0.6 0.0 copy-start
  0.6 1.1 %copy-done = bf16[9,128,256]{2,1,0:T(8,128)(2,1)S(1)} copy-done((bf16[9,128,256]{2,1,0:T(8,128)(2,1)S(1)}, bf16[9,128,256]{2,1,0:T(8,128)(2,1)}, u32[]{:S(2)}) %copy-start) | copy-done | bytes 589848
  1.7 0.0 copy-start.1
  1.7 0.9 %copy-done.1 = bf16[9,32,7,9]{1,2,3,0:T(8,128)(2,1)S(1)} copy-done((bf16[9,32,7,9]{1,2,3,0:T(8,128)(2,1)S(1)}, bf16[9,32,7,9]{1,2,3,0:T(8,128)(2,1)}, u32[]{:S(2)}) %copy-start.1) | copy-done | bytes 36312
  2.6 0.0 copy-start.2
  2.6 0.8 %copy-done.2 = bf16[16,16,128]{2,1,0:T(8,128)(2,1)S(1)} copy-done((bf16[16,16,128]{2,1,0:T(8,128)(2,1)S(1)}, bf16[16,16,128]{2,1,0:T(8,128)(2,1)}, u32[]{:S(2)}) %copy-start.2) | copy-done | bytes 65560
  3.5 0.0 copy-start.3
  3.5 0.8 %copy-done.3 = bf16[16,16,128]{2,1,0:T(8,128)(2,1)S(1)} copy-done((bf16[16,16,128]{2,1,0:T(8,128)(2,1)S(1)}, bf16[16,16,128]{2,1,0:T(8,128)(2,1)}, u32[]{:S(2)}) %copy-start.3) | copy-done | bytes 65560
  4.3 0.0 copy-start.4
  4.3 0.7 %copy-done.4 = s32[32,7]{0,1:T(8,128)S(1)} copy-done((s32[32,7]{0,1:T(8,128)S(1)}, s32[32,7]{0,1:T(8,128)}, u32[]{:S(2)}) %copy-start.4) | copy-done | bytes 920
  5.0 0.0 copy-start.5
  5.0 0.7 %copy-done.5 = s32[32]{0:T(128)S(1)} copy-done((s32[32]{0:T(128)S(1)}, s32[32]{0:T(128)}, u32[]{:S(2)}) %copy-start.5) | copy-done | bytes 152
  5.6 32.9 %shard_map.85 = (bf16[16,16,128]{2,1,0:T(8,128)(2,1)S(1)}, bf16[16,16,128]{2,1,0:T(8,128)(2,1)S(1)}, bf16[2,4,144,256]{3,2,1,0:T(8,128)(2,1)S(1)}) custom-call(bf16[16,16,128]{2,1,0:T(8,128)(2,1)S(1)} %copy-done.2, bf16[9,9,7,32]{3,2,1,0:T(8,128)(2,1)S(1)} %bitcast.6, s32[7,32]{1,0:T(8,128)S(1)} %bitcast.7, s32[1,32]{1,0:T(1,128)S(1)} %bitcast.8, ...), custom_call_target="tpu_custom_call" | custom-call | tf_op jit(solution)/shard_map/pallas_call | solution.py:388
  38.5 1.1 %convert.1 = f32[9,128,256]{2,1,0:T(8,128)} convert(bf16[9,128,256]{2,1,0:T(8,128)(2,1)S(1)} %bitcast.5) | non-fusion elementwise | flops 294912 | bytes 1769472 | tf_op jit(solution)/shard_map/convert_element_type | solution.py:449
  39.6 0.6 %copy.11 = bf16[16,16,128]{2,1,0:T(8,128)(2,1)} copy(bf16[16,16,128]{2,1,0:T(8,128)(2,1)S(1)} %get-tuple-element.12) | data formatting | bytes 131072
  40.3 0.6 %copy.12 = bf16[16,16,128]{2,1,0:T(8,128)(2,1)} copy(bf16[16,16,128]{2,1,0:T(8,128)(2,1)S(1)} %get-tuple-element.13) | data formatting | bytes 131072
Async XLA Ops:
  0.6 1.1 %copy-start = (bf16[9,128,256]{2,1,0:T(8,128)(2,1)S(1)}, bf16[9,128,256]{2,1,0:T(8,128)(2,1)}, u32[]{:S(2)}) copy-start(bf16[9,128,256]{2,1,0:T(8,128)(2,1)} %weight.1) | copy-start | bytes 1769476
  1.7 0.9 %copy-start.1 = (bf16[9,32,7,9]{1,2,3,0:T(8,128)(2,1)S(1)}, bf16[9,32,7,9]{1,2,3,0:T(8,128)(2,1)}, u32[]{:S(2)}) copy-start(bf16[9,32,7,9]{1,2,3,0:T(8,128)(2,1)} %param.7) | copy-start | bytes 108868
  2.6 0.8 %copy-start.2 = (bf16[16,16,128]{2,1,0:T(8,128)(2,1)S(1)}, bf16[16,16,128]{2,1,0:T(8,128)(2,1)}, u32[]{:S(2)}) copy-start(bf16[16,16,128]{2,1,0:T(8,128)(2,1)} %feat.1) | copy-start | bytes 196612
  3.5 0.8 %copy-start.3 = (bf16[16,16,128]{2,1,0:T(8,128)(2,1)S(1)}, bf16[16,16,128]{2,1,0:T(8,128)(2,1)}, u32[]{:S(2)}) copy-start(bf16[16,16,128]{2,1,0:T(8,128)(2,1)} %cot.1) | copy-start | bytes 196612
  4.3 0.7 %copy-start.4 = (s32[32,7]{0,1:T(8,128)S(1)}, s32[32,7]{0,1:T(8,128)}, u32[]{:S(2)}) copy-start(s32[32,7]{0,1:T(8,128)} %param.8) | copy-start | bytes 2692
  5.0 0.7 %copy-start.5 = (s32[32]{0:T(128)S(1)}, s32[32]{0:T(128)}, u32[]{:S(2)}) copy-start(s32[32]{0:T(128)} %param.9) | copy-start | bytes 388

commit v3 on v2

--- a/solution.py
+++ b/solution.py
@@ -11,6 +11,7 @@
 QS = 32
 BF = jnp.bfloat16
 F32 = jnp.float32
+GRANT = 63 * 1024 * 1024
 
 
 def dot(a, b, ca, cb):
@@ -19,15 +20,26 @@
 
 def kernel(
     dims,
+    feat_hbm,
+    basis_hbm,
+    active_hbm,
+    reach_hbm,
+    weight_hbm,
+    cot_hbm,
+    out_hbm,
+    igrad_hbm,
+    wg_hbm,
+    out,
+    igrad,
+    wg,
+    s_out,
     feat,
     basis,
     active,
     reach,
     weight,
     cot,
-    out,
-    igrad,
-    wg,
+    s_in,
     base,
     ext,
     acc,
@@ -81,7 +93,13 @@
 
     mate = (ens, n, l, 1 - ch)
     lats = [lax.rem(l + d, L) for d in range(1, L)]
-    lons = [lax.rem(n + d, N) for d in range(1, N)]
+    low = n < N // 2
+    lons = []
+    for step in range(N - 1):
+        down, up = N - 1 - step, step
+        down = jnp.where(down <= n, down - 1, down)
+        up = jnp.where(up >= n, up + 1, up)
+        lons.append(jnp.where(low, down, up))
 
     def remote(src, dst, ss, rs, device):
         return pltpu.make_async_remote_copy(
@@ -105,11 +123,27 @@
             greet(dev(lat, left))
             greet(dev(lat, right))
 
+    pairs = (
+        (feat_hbm, feat),
+        (cot_hbm, cot),
+        (basis_hbm, basis),
+        (active_hbm, active),
+        (reach_hbm, reach),
+        (weight_hbm, weight),
+    )
+    loads = [pltpu.make_async_copy(src, dst, s_in.at[i]) for i, (src, dst) in enumerate(pairs)]
+    for load in loads:
+        load.start()
+    loads[0].wait()
+
     for r in range(R):
         row = feat[r].astype(F32)
         fpk[0, 4 * r : 4 * r + 4] = row[:lon_half]
         fpk[1, 4 * r : 4 * r + 4] = row[J - lon_half :]
     edge[...] = fpk[...].astype(BF)
+
+    for load in loads[2:5]:
+        load.wait()
 
     A, B = basis.shape[2], basis.shape[1]
     where = lax.broadcasted_iota(jnp.int32, (8 * B, 8 * QS), 0)
@@ -136,12 +170,11 @@
 
     lax.fori_loop(0, R, make_tiles, 0, unroll=4)
 
-    cotf[ch] = cot[...]
     ext[...] = jnp.zeros_like(ext)
     acc[...] = jnp.zeros_like(acc)
-
     for r in range(R):
         ext[r + half, 8 : 8 + J] = feat[r].astype(F32)
+
 
     corners = 2 * (has_up.astype(jnp.int32) + has_down.astype(jnp.int32))
     pl.semaphore_wait(barrier, 1 + (L - 1) + (N - 1) + corners)
@@ -188,13 +221,16 @@
         s_f,
         r_f,
     )
+    loads[1].wait()
     cot_copy = remote(cot, cotf.at[ch], s_ch.at[0], r_ch.at[0], mate)
     each(fwd, lambda c: c.start())
     cot_copy.start()
+    cotf[ch] = cot[...]
 
     def recv_wait(dst, sem):
         remote(dst, dst, sem, sem, mate).wait_recv()
 
+    loads[5].wait()
     cot_copy.wait_recv()
     cot_full = jnp.concatenate(
         [cotf[0].reshape(cells, C), cotf[1].reshape(cells, C)], axis=1
@@ -208,8 +244,6 @@
         part = dot(tiles[i], spread[i], 0, 0)
         acc[pl.ds(i, 8)] += part.reshape(8, QS, C)
         return _
-
-    lax.fori_loop(0, R // 2, back, 0, unroll=4)
 
     for side in (0, 1):
         recv_wait(ein.at[side], r_f.at[side])
@@ -282,7 +316,11 @@
     out_copy = remote(pout.at[1 - ch], pin, s_ch.at[1], r_ch.at[1], mate)
     out_copy.start()
 
+    lax.fori_loop(0, R // 2, back, 0, unroll=4)
+    pass_on(lons[0])
     lax.fori_loop(R // 2, R, back, 0, unroll=4)
+    for c in lons[1:2]:
+        pass_on(c)
 
     gpk[...] = jnp.zeros_like(gpk)
     for side in (0, 1):
@@ -305,7 +343,7 @@
     )
     each(bwd, lambda c: c.start())
 
-    for c in lons:
+    for c in lons[2:]:
         pass_on(c)
     zown[...] = lat_sum(n)
 
@@ -328,6 +366,8 @@
 
     out_copy.wait_recv()
     out[...] = (pout[ch] + pin[...]).astype(BF).reshape(R, J, C)
+    results = [pltpu.make_async_copy(out, out_hbm, s_out.at[0])]
+    results[-1].start()
 
     for side in (0, 1):
         recv_wait(gin.at[side], r_g.at[side])
@@ -351,15 +391,28 @@
                     acc[first + r, at : at + lon_half] += cols[4 * r : 4 * r + 4]
     for r in range(R):
         igrad[r] = acc[r + half, 8 : 8 + J].astype(BF)
-
-    for c in lons:
+    results.append(pltpu.make_async_copy(igrad, igrad_hbm, s_out.at[1]))
+    results[-1].start()
+
+    def chunk_out(lat, c, at):
+        results.append(pltpu.make_async_copy(wg.at[lat, c], wg_hbm.at[lat, c], s_out.at[at]))
+        results[-1].start()
+
+    chunk_out(l, n, 2)
+
+    near = lons[::-1]
+    for i, c in enumerate(near):
         recv_wait(wg.at[l, c], r_az.at[c])
         for lat in lats:
             ax_copy(lat, c).start()
-    for c in [n] + lons:
-        for lat in lats:
+        chunk_out(l, c, 3 + i)
+    for i, c in enumerate([n] + near):
+        for j, lat in enumerate(lats):
             recv_wait(wg.at[lat, c], r_ax.at[lat, c])
-
+            chunk_out(lat, c, 2 + N + (L - 1) * i + j)
+
+    for result in results:
+        result.wait()
     cot_copy.wait_send()
     out_copy.wait_send()
     each(fwd, lambda c: c.wait_send())
@@ -383,7 +436,6 @@
     pc = -(-per_lat // (16 * N)) * 16
     cells = R * J
 
-    vmem = pl.BlockSpec(memory_space=pltpu.VMEM)
     dma = pltpu.SemaphoreType.DMA
     output, input_grad, wg = pl.pallas_call(
         functools.partial(kernel, (L, N, half, lon_half, per_lat, pc)),
@@ -392,9 +444,20 @@
             jax.ShapeDtypeStruct((R, J, C), BF),
             jax.ShapeDtypeStruct((L, N, pc, O), BF),
         ),
-        in_specs=[vmem] * 6,
-        out_specs=(vmem,) * 3,
+        in_specs=[pl.BlockSpec(memory_space=pltpu.HBM)] * 6,
+        out_specs=(pl.BlockSpec(memory_space=pltpu.HBM),) * 3,
         scratch_shapes=[
+            pltpu.VMEM((R, J, C), BF),
+            pltpu.VMEM((R, J, C), BF),
+            pltpu.VMEM((L, N, pc, O), BF),
+            dma((2 + L * N,)),
+            pltpu.VMEM((R, J, C), BF),
+            pltpu.VMEM((K, lon_span, lat_span, rows), BF),
+            pltpu.VMEM((lat_span, rows), jnp.int32),
+            pltpu.VMEM((1, rows), jnp.int32),
+            pltpu.VMEM((K, C, O), BF),
+            pltpu.VMEM((R, J, C), BF),
+            dma((6,)),
             pltpu.VMEM((K, rows, 8 * QS), F32),
             pltpu.VMEM((R + 8, QS, C), F32),
             pltpu.VMEM((R + 8, QS, C), F32),
@@ -436,7 +499,7 @@
             dma((L, N)),
         ],
         compiler_params=pltpu.CompilerParams(
-            collective_id=0, has_side_effects=True, vmem_limit_bytes=40 * 1024 * 1024
+            collective_id=0, has_side_effects=True, vmem_limit_bytes=GRANT
         ),
     )(
         features,

time: 41.2 us -> 37.9 us (0.920)
  local copies, waits for them, and re-layouts: 6.25 us -> 1.27 us
  other arithmetic: 1.13 us -> 2.22 us
  Pallas kernels: 32.9 us -> 33.6 us
    unnamed x14 -> x6, local copies, waits for them, and re-layouts: 6.25 us -> 1.27 us
    convert_element_type x1, other arithmetic: 1.13 us -> 2.22 us  [body(): wg.reshape(L, N * pc, O)[:, :per_lat].reshape(K, C, O).astype(F32)]
    pallas_call x1, Pallas kernels: 32.9 us -> 33.6 us  [body(): pl.pallas_call(functools.partial(kernel, (L, N, half, lon_half, per_lat,...]
where the time goes in v3:
time: 37.9 us; the launch traced here: 37.7 us
  Pallas kernels  33.6 us (89%)
  other arithmetic  2.22 us (6%)
  local copies, waits for them, and re-layouts  1.27 us (3%)
  between operations  0.66 us (2%)
    pallas_call x1, Pallas kernels, body(): pl.pallas_call(functools.partial(kernel, (L, N, half, lon_half, per_lat,...  33.6 us
    convert_element_type x1, other arithmetic, body(): wg.reshape(L, N * pc, O)[:, :per_lat].reshape(K, C, O).astype(F32)  2.22 us
    unnamed x6, local copies, waits for them, and re-layouts  1.27 us

profile of v3, /device:TPU:0, one launch (start us, length us, event | category | flops | bytes accessed | tf_op | source)
XLA Modules:
  0.0 37.7 jit_solution(6913080056573701727)
XLA Ops:
  0.6 33.6 %shard_map.85 = (bf16[16,16,128]{2,1,0:T(8,128)(2,1)}, bf16[16,16,128]{2,1,0:T(8,128)(2,1)}, bf16[2,4,144,256]{3,2,1,0:T(8,128)(2,1)}) custom-call(bf16[16,16,128]{2,1,0:T(8,128)(2,1)} %feat_hbm.1, bf16[9,9,7,32]{3,2,1,0:T(8,128)(2,1)} %bitcast.6, s32[7,32]{1,0:T(8,128)} %bitcast.7, s32[1,32]{1,0:T(1,128)} %bitcast.8, bf16[9,128,256]{2,1,0:T(8,128)(2,1)} %weight_hbm.1, ...), custom_call_target="tpu_custom_call" | custom-call | tf_op jit(solution)/shard_map/pallas_call | solution.py:440
  34.2 0.0 copy-start.1
  34.2 0.0 copy-start
  34.2 2.2 %convert.1 = f32[9,128,256]{2,1,0:T(8,128)} convert(bf16[9,128,256]{2,1,0:T(8,128)(2,1)} %bitcast.5) | non-fusion elementwise | flops 294912 | bytes 1769472 | tf_op jit(solution)/shard_map/convert_element_type | solution.py:512
  36.5 0.0 copy-done.1
  36.5 0.6 %copy.11 = bf16[16,16,128]{2,1,0:T(8,128)(2,1)} copy(bf16[16,16,128]{2,1,0:T(8,128)(2,1)S(1)} %copy-done.1) | data formatting | bytes 131072
  37.1 0.0 copy-done
  37.1 0.6 %copy.12 = bf16[16,16,128]{2,1,0:T(8,128)(2,1)} copy(bf16[16,16,128]{2,1,0:T(8,128)(2,1)S(1)} %copy-done) | data formatting | bytes 131072
Async XLA Ops:
  34.2 2.2 %copy-start.1 = (bf16[16,16,128]{2,1,0:T(8,128)(2,1)S(1)}, bf16[16,16,128]{2,1,0:T(8,128)(2,1)}, u32[]{:S(2)}) copy-start(bf16[16,16,128]{2,1,0:T(8,128)(2,1)} %get-tuple-element.12) | copy-start | bytes 196612
  34.2 2.9 %copy-start = (bf16[16,16,128]{2,1,0:T(8,128)(2,1)S(1)}, bf16[16,16,128]{2,1,0:T(8,128)(2,1)}, u32[]{:S(2)}) copy-start(bf16[16,16,128]{2,1,0:T(8,128)(2,1)} %get-tuple-element.13) | copy-start | bytes 196612

commit v4 on v3

--- a/solution.py
+++ b/solution.py
@@ -42,6 +42,7 @@
     s_in,
     base,
     ext,
+    extb,
     acc,
     tiles,
     mixed,
@@ -111,17 +112,18 @@
     def greet(device):
         pl.semaphore_signal(barrier, inc=1, device_id=device, device_id_type=MESH)
 
-    greet(mate)
-    for lat in lats:
-        greet(dev(lat, n))
-    for lon in lons:
-        greet(dev(l, lon))
     for has, lat in ((has_up, l - 1), (has_down, l + 1)):
 
         @pl.when(has)
         def _():
             greet(dev(lat, left))
             greet(dev(lat, right))
+
+    for lon in lons:
+        greet(dev(l, lon))
+    for lat in lats:
+        greet(dev(lat, n))
+    greet(mate)
 
     pairs = (
         (feat_hbm, feat),
@@ -201,6 +203,13 @@
 
     def each(copies, action):
         lon_copy, corner, lat_copy = copies
+        for down, has in ((0, has_up), (1, has_down)):
+
+            @pl.when(has)
+            def _():
+                for side in (0, 1):
+                    action(corner(side, down))
+
         for side in (0, 1):
             action(lon_copy(side))
         for down, has in ((0, has_up), (1, has_down)):
@@ -208,8 +217,6 @@
             @pl.when(has)
             def _():
                 action(lat_copy(down))
-                for side in (0, 1):
-                    action(corner(side, down))
 
     fwd = edge_copies(
         lambda s: edge.at[s],
@@ -245,6 +252,8 @@
         acc[pl.ds(i, 8)] += part.reshape(8, QS, C)
         return _
 
+    lax.fori_loop(0, R // 2, back, 0, unroll=4)
+
     for side in (0, 1):
         recv_wait(ein.at[side], r_f.at[side])
         cols = ein[side].astype(F32)
@@ -267,8 +276,10 @@
                 for r in range(half):
                     ext[first + r, at : at + lon_half] = cols[skip + 4 * r : skip + 4 * r + 4]
 
+    extb[...] = ext[...].astype(BF)
+
     def mix(i, _):
-        window = ext[pl.ds(i, 8)].reshape(8 * QS, C).astype(BF)
+        window = extb[pl.ds(i, 8)].reshape(8 * QS, C)
         row = dot(tiles[i], window, 1, 0).astype(BF)
         for k in range(K):
             mixed[k, pl.ds(pl.multiple_of(i * J, J), J)] = row[J * k : J * k + J]
@@ -276,37 +287,63 @@
 
     lax.fori_loop(0, R, mix, 0, unroll=4)
 
-    for k in range(K):
+    start_k = (lats + [l])[0] * per_lat // C
+
+    def grad(step):
+        k = lax.rem(start_k + step, K)
         g = dot(mixed[k], cot_full, 0, 0)
-        gf[C * k : C * k + C] = g
-        gb[C * k : C * k + C] = g.astype(BF)
-
-    def rows(lat, c):
-        start = lat * per_lat + jnp.minimum(c * pc, per_lat - pc)
-        return pl.ds(pl.multiple_of(start, 16), pc)
+        at = pl.ds(pl.multiple_of(k * C, C), C)
+        gf[at] = g
+        gb[at] = g.astype(BF)
+
+    head = -(-per_lat // C) + (0 if per_lat % C == 0 or L == 2 else 1)
+    for step in range(head):
+        grad(step)
+
+    cut = -(-pc // 32) * 16
+    pieces = [(0, cut), (cut, pc - cut)] if pc > cut else [(0, pc)]
+
+    def part(p):
+        return pl.ds(pieces[p][0], pieces[p][1])
+
+    def rows(lat, c, p):
+        start = lat * per_lat + jnp.minimum(c * pc, per_lat - pc) + pieces[p][0]
+        return pl.ds(pl.multiple_of(start, 16), pieces[p][1])
+
+    P2 = range(len(pieces))
 
     order = lons + [n]
 
-    def rx_copy(lat, c):
-        return remote(gb.at[rows(lat, c)], rx.at[l, c], s_rx.at[lat, c], r_rx.at[l, c], dev(lat, n))
+    def rx_copy(lat, c, p):
+        return remote(
+            gb.at[rows(lat, c, p)], rx.at[l, c, part(p)], s_rx.at[lat, c, p], r_rx.at[l, c, p], dev(lat, n)
+        )
 
     for c in order:
+        for lat in lats[:1]:
+            for p in P2:
+                rx_copy(lat, c, p).start()
+    for step in range(head, K):
+        grad(step)
+    for c in order:
+        for lat in lats[1:]:
+            for p in P2:
+                rx_copy(lat, c, p).start()
+
+    def rz_copy(c, p):
+        return remote(zb.at[c, part(p)], rz.at[n, part(p)], s_rz.at[c, p], r_rz.at[n, p], dev(l, c))
+
+    def lat_sum(c, p):
+        total = gf[rows(l, c, p)]
         for lat in lats:
-            rx_copy(lat, c).start()
-
-    def rz_copy(c):
-        return remote(zb.at[c], rz.at[n], s_rz.at[c], r_rz.at[n], dev(l, c))
-
-    def lat_sum(c):
-        total = gf[rows(l, c)]
-        for lat in lats:
-            recv_wait(rx.at[lat, c], r_rx.at[lat, c])
-            total = total + rx[lat, c].astype(F32)
+            recv_wait(rx.at[lat, c, part(p)], r_rx.at[lat, c, p])
+            total = total + rx[lat, c, part(p)].astype(F32)
         return total
 
     def pass_on(c):
-        zb[c] = lat_sum(c).astype(BF)
-        rz_copy(c).start()
+        for p in P2:
+            zb[c, part(p)] = lat_sum(c, p).astype(BF)
+            rz_copy(c, p).start()
 
     total = dot(mixed[0], weight[0], 1, 0)
     for k in range(1, K):
@@ -316,11 +353,7 @@
     out_copy = remote(pout.at[1 - ch], pin, s_ch.at[1], r_ch.at[1], mate)
     out_copy.start()
 
-    lax.fori_loop(0, R // 2, back, 0, unroll=4)
-    pass_on(lons[0])
     lax.fori_loop(R // 2, R, back, 0, unroll=4)
-    for c in lons[1:2]:
-        pass_on(c)
 
     gpk[...] = jnp.zeros_like(gpk)
     for side in (0, 1):
@@ -343,26 +376,30 @@
     )
     each(bwd, lambda c: c.start())
 
-    for c in lons[2:]:
+    for c in lons:
         pass_on(c)
-    zown[...] = lat_sum(n)
-
-    total = zown[...]
-    for c in lons:
-        recv_wait(rz.at[c], r_rz.at[c])
-        total = total + rz[c].astype(F32)
-    wg[l, n] = total.astype(BF)
-
-    def az_copy(lon):
-        return remote(wg.at[l, n], wg.at[l, n], s_az.at[lon], r_az.at[n], dev(l, lon))
-
-    def ax_copy(lat, c):
-        return remote(wg.at[l, c], wg.at[l, c], s_ax.at[lat, c], r_ax.at[l, c], dev(lat, n))
-
-    for lon in lons:
-        az_copy(lon).start()
-    for lat in lats:
-        ax_copy(lat, n).start()
+    for p in P2:
+        zown[part(p)] = lat_sum(n, p)
+
+    def az_copy(lon, p):
+        here = wg.at[l, n, part(p)]
+        return remote(here, here, s_az.at[lon, p], r_az.at[n, p], dev(l, lon))
+
+    def ax_copy(lat, c, p):
+        return remote(
+            wg.at[l, c, part(p)], wg_hbm.at[l, c, part(p)], s_ax.at[lat, c, p], r_ax.at[l, c, p], dev(lat, n)
+        )
+
+    for p in P2:
+        total = zown[part(p)]
+        for c in lons[::-1]:
+            recv_wait(rz.at[c, part(p)], r_rz.at[c, p])
+            total = total + rz[c, part(p)].astype(F32)
+        wg[l, n, part(p)] = total.astype(BF)
+        for lon in lons:
+            az_copy(lon, p).start()
+        for lat in lats:
+            ax_copy(lat, n, p).start()
 
     out_copy.wait_recv()
     out[...] = (pout[ch] + pin[...]).astype(BF).reshape(R, J, C)
@@ -402,14 +439,15 @@
 
     near = lons[::-1]
     for i, c in enumerate(near):
-        recv_wait(wg.at[l, c], r_az.at[c])
+        for p in P2:
+            recv_wait(wg.at[l, c, part(p)], r_az.at[c, p])
+            for lat in lats:
+                ax_copy(lat, c, p).start()
+        chunk_out(l, c, 3 + i)
+    for c in [n] + near:
         for lat in lats:
-            ax_copy(lat, c).start()
-        chunk_out(l, c, 3 + i)
-    for i, c in enumerate([n] + near):
-        for j, lat in enumerate(lats):
-            recv_wait(wg.at[lat, c], r_ax.at[lat, c])
-            chunk_out(lat, c, 2 + N + (L - 1) * i + j)
+            for p in P2:
+                recv_wait(wg_hbm.at[lat, c, part(p)], r_ax.at[lat, c, p])
 
     for result in results:
         result.wait()
@@ -418,12 +456,14 @@
     each(fwd, lambda c: c.wait_send())
     each(bwd, lambda c: c.wait_send())
     for c in lons:
-        rz_copy(c).wait_send()
-        az_copy(c).wait_send()
+        for p in P2:
+            rz_copy(c, p).wait_send()
+            az_copy(c, p).wait_send()
     for c in order:
         for lat in lats:
-            rx_copy(lat, c).wait_send()
-            ax_copy(lat, c).wait_send()
+            for p in P2:
+                rx_copy(lat, c, p).wait_send()
+                ax_copy(lat, c, p).wait_send()
 
 
 def body(features, basis, active, reach, weight, cotangent):
@@ -450,7 +490,7 @@
             pltpu.VMEM((R, J, C), BF),
             pltpu.VMEM((R, J, C), BF),
             pltpu.VMEM((L, N, pc, O), BF),
-            dma((2 + L * N,)),
+            dma((2 + N,)),
             pltpu.VMEM((R, J, C), BF),
             pltpu.VMEM((K, lon_span, lat_span, rows), BF),
             pltpu.VMEM((lat_span, rows), jnp.int32),
@@ -460,6 +500,7 @@
             dma((6,)),
             pltpu.VMEM((K, rows, 8 * QS), F32),
             pltpu.VMEM((R + 8, QS, C), F32),
+            pltpu.VMEM((R + 8, QS, C), BF),
             pltpu.VMEM((R + 8, QS, C), F32),
             pltpu.VMEM((R, K * J, 8 * QS), BF),
             pltpu.VMEM((K, cells, C), BF),
@@ -489,14 +530,14 @@
             dma((8,)),
             dma((8,)),
             dma((8,)),
-            dma((L, N)),
-            dma((L, N)),
-            dma((N,)),
-            dma((N,)),
-            dma((N,)),
-            dma((N,)),
-            dma((L, N)),
-            dma((L, N)),
+            dma((L, N, 2)),
+            dma((L, N, 2)),
+            dma((N, 2)),
+            dma((N, 2)),
+            dma((N, 2)),
+            dma((N, 2)),
+            dma((L, N, 2)),
+            dma((L, N, 2)),
         ],
         compiler_params=pltpu.CompilerParams(
             collective_id=0, has_side_effects=True, vmem_limit_bytes=GRANT

time: 37.9 us -> 36.2 us (0.955)
  Pallas kernels: 33.6 us -> 31.9 us
    pallas_call x1, Pallas kernels: 33.6 us -> 31.9 us  [body(): pl.pallas_call(functools.partial(kernel, (L, N, half, lon_half, per_lat,...]
where the time goes in v4:
time: 36.2 us; the launch traced here: 36.1 us
  Pallas kernels  31.9 us (88%)
  other arithmetic  2.22 us (6%)
  local copies, waits for them, and re-layouts  1.27 us (4%)
  between operations  0.66 us (2%)
    pallas_call x1, Pallas kernels, body(): pl.pallas_call(functools.partial(kernel, (L, N, half, lon_half, per_lat,...  31.9 us
    convert_element_type x1, other arithmetic, body(): wg.reshape(L, N * pc, O)[:, :per_lat].reshape(K, C, O).astype(F32)  2.22 us
    unnamed x6, local copies, waits for them, and re-layouts  1.27 us

profile of v4, /device:TPU:0, one launch (start us, length us, event | category | flops | bytes accessed | tf_op | source)
XLA Modules:
  0.0 36.1 jit_solution(10727487150703197005)
XLA Ops:
  0.6 31.9 %shard_map.85 = (bf16[16,16,128]{2,1,0:T(8,128)(2,1)}, bf16[16,16,128]{2,1,0:T(8,128)(2,1)}, bf16[2,4,144,256]{3,2,1,0:T(8,128)(2,1)}) custom-call(bf16[16,16,128]{2,1,0:T(8,128)(2,1)} %feat_hbm.1, bf16[9,9,7,32]{3,2,1,0:T(8,128)(2,1)} %bitcast.6, s32[7,32]{1,0:T(8,128)} %bitcast.7, s32[1,32]{1,0:T(1,128)} %bitcast.8, bf16[9,128,256]{2,1,0:T(8,128)(2,1)} %weight_hbm.1, ...), custom_call_target="tpu_custom_call" | custom-call | tf_op jit(solution)/shard_map/pallas_call | solution.py:480
  32.6 0.0 copy-start.1
  32.6 0.0 copy-start
  32.6 2.2 %convert.1 = f32[9,128,256]{2,1,0:T(8,128)} convert(bf16[9,128,256]{2,1,0:T(8,128)(2,1)} %bitcast.5) | non-fusion elementwise | flops 294912 | bytes 1769472 | tf_op jit(solution)/shard_map/convert_element_type | solution.py:553
  34.8 0.0 copy-done.1
  34.8 0.6 %copy.11 = bf16[16,16,128]{2,1,0:T(8,128)(2,1)} copy(bf16[16,16,128]{2,1,0:T(8,128)(2,1)S(1)} %copy-done.1) | data formatting | bytes 131072
  35.4 0.0 copy-done
  35.4 0.6 %copy.12 = bf16[16,16,128]{2,1,0:T(8,128)(2,1)} copy(bf16[16,16,128]{2,1,0:T(8,128)(2,1)S(1)} %copy-done) | data formatting | bytes 131072
Async XLA Ops:
  32.6 2.2 %copy-start.1 = (bf16[16,16,128]{2,1,0:T(8,128)(2,1)S(1)}, bf16[16,16,128]{2,1,0:T(8,128)(2,1)}, u32[]{:S(2)}) copy-start(bf16[16,16,128]{2,1,0:T(8,128)(2,1)} %get-tuple-element.12) | copy-start | bytes 196612
  32.6 2.9 %copy-start = (bf16[16,16,128]{2,1,0:T(8,128)(2,1)S(1)}, bf16[16,16,128]{2,1,0:T(8,128)(2,1)}, u32[]{:S(2)}) copy-start(bf16[16,16,128]{2,1,0:T(8,128)(2,1)} %get-tuple-element.13) | copy-start | bytes 196612

commit v5 on v4

--- a/solution.py
+++ b/solution.py
@@ -170,7 +170,7 @@
                 tiles[i, J * k : J * k + J, 128 * h : 128 * h + 128] = turned.astype(BF)
         return _
 
-    lax.fori_loop(0, R, make_tiles, 0, unroll=4)
+    lax.fori_loop(0, R, make_tiles, 0, unroll=8)
 
     ext[...] = jnp.zeros_like(ext)
     acc[...] = jnp.zeros_like(acc)
@@ -252,8 +252,6 @@
         acc[pl.ds(i, 8)] += part.reshape(8, QS, C)
         return _
 
-    lax.fori_loop(0, R // 2, back, 0, unroll=4)
-
     for side in (0, 1):
         recv_wait(ein.at[side], r_f.at[side])
         cols = ein[side].astype(F32)
@@ -285,7 +283,7 @@
             mixed[k, pl.ds(pl.multiple_of(i * J, J), J)] = row[J * k : J * k + J]
         return _
 
-    lax.fori_loop(0, R, mix, 0, unroll=4)
+    lax.fori_loop(0, R, mix, 0, unroll=8)
 
     start_k = (lats + [l])[0] * per_lat // C
 
@@ -353,7 +351,7 @@
     out_copy = remote(pout.at[1 - ch], pin, s_ch.at[1], r_ch.at[1], mate)
     out_copy.start()
 
-    lax.fori_loop(R // 2, R, back, 0, unroll=4)
+    lax.fori_loop(0, R, back, 0, unroll=8)
 
     gpk[...] = jnp.zeros_like(gpk)
     for side in (0, 1):

time: 36.2 us -> 35.6 us (0.983)
  Pallas kernels: 31.9 us -> 31.3 us
    pallas_call x1, Pallas kernels: 31.9 us -> 31.3 us  [body(): pl.pallas_call(functools.partial(kernel, (L, N, half, lon_half, per_lat,...]
where the time goes in v5:
time: 35.6 us; the launch traced here: 35.5 us
  Pallas kernels  31.3 us (88%)
  other arithmetic  2.22 us (6%)
  local copies, waits for them, and re-layouts  1.27 us (4%)
  between operations  0.66 us (2%)
    pallas_call x1, Pallas kernels, body(): pl.pallas_call(functools.partial(kernel, (L, N, half, lon_half, per_lat,...  31.3 us
    convert_element_type x1, other arithmetic, body(): wg.reshape(L, N * pc, O)[:, :per_lat].reshape(K, C, O).astype(F32)  2.22 us
    unnamed x6, local copies, waits for them, and re-layouts  1.27 us

profile of v5, /device:TPU:0, one launch (start us, length us, event | category | flops | bytes accessed | tf_op | source)
XLA Modules:
  0.0 35.5 jit_solution(9060883958876505867)
XLA Ops:
  0.6 31.3 %shard_map.85 = (bf16[16,16,128]{2,1,0:T(8,128)(2,1)}, bf16[16,16,128]{2,1,0:T(8,128)(2,1)}, bf16[2,4,144,256]{3,2,1,0:T(8,128)(2,1)}) custom-call(bf16[16,16,128]{2,1,0:T(8,128)(2,1)} %feat_hbm.1, bf16[9,9,7,32]{3,2,1,0:T(8,128)(2,1)} %bitcast.6, s32[7,32]{1,0:T(8,128)} %bitcast.7, s32[1,32]{1,0:T(1,128)} %bitcast.8, bf16[9,128,256]{2,1,0:T(8,128)(2,1)} %weight_hbm.1, ...), custom_call_target="tpu_custom_call" | custom-call | tf_op jit(solution)/shard_map/pallas_call | solution.py:478
  32.0 0.0 copy-start.1
  32.0 0.0 copy-start
  32.0 2.2 %convert.1 = f32[9,128,256]{2,1,0:T(8,128)} convert(bf16[9,128,256]{2,1,0:T(8,128)(2,1)} %bitcast.5) | non-fusion elementwise | flops 294912 | bytes 1769472 | tf_op jit(solution)/shard_map/convert_element_type | solution.py:551
  34.2 0.0 copy-done.1
  34.2 0.6 %copy.11 = bf16[16,16,128]{2,1,0:T(8,128)(2,1)} copy(bf16[16,16,128]{2,1,0:T(8,128)(2,1)S(1)} %copy-done.1) | data formatting | bytes 131072
  34.8 0.0 copy-done
  34.8 0.6 %copy.12 = bf16[16,16,128]{2,1,0:T(8,128)(2,1)} copy(bf16[16,16,128]{2,1,0:T(8,128)(2,1)S(1)} %copy-done) | data formatting | bytes 131072
Async XLA Ops:
  32.0 2.2 %copy-start.1 = (bf16[16,16,128]{2,1,0:T(8,128)(2,1)S(1)}, bf16[16,16,128]{2,1,0:T(8,128)(2,1)}, u32[]{:S(2)}) copy-start(bf16[16,16,128]{2,1,0:T(8,128)(2,1)} %get-tuple-element.12) | copy-start | bytes 196612
  32.0 2.9 %copy-start = (bf16[16,16,128]{2,1,0:T(8,128)(2,1)S(1)}, bf16[16,16,128]{2,1,0:T(8,128)(2,1)}, u32[]{:S(2)}) copy-start(bf16[16,16,128]{2,1,0:T(8,128)(2,1)} %get-tuple-element.13) | copy-start | bytes 196612
